TPU v7x, 32 devices: a whole 2x2x4 slice. The times are simulated.
32 devices in a mesh: groups: 2 (over y), wide: 16 (over z, x, core).
Axes of the slice: x: 2, y: 2, z: 4, core: 2. Of those that a mesh axis runs over, the one named last changes fastest.
Arguments:
- fields: bfloat16 [32, 512], P(('groups', 'wide')), parts along dimension 0, may hold values from -6 to 6
- chol: bfloat16 [512, 1024, 1024], P(None, 'wide'), may hold values from -0.01171875 to 0.01171875
- orbitals: bfloat16 [32, 1024, 256], P(('groups', 'wide')), parts along dimension 0, may hold values from -6 to 6
- trial: bfloat16 [1024, 256], replicated, may hold values from -0.5 to 0.5
Outputs:
- new_orbitals: bfloat16 [32, 1024, 256], P(('groups', 'wide')), parts along dimension 0
- force_bias: float32 [32, 2, 512], P(('groups', 'wide')), parts along dimension 0
There are 2 independent parts, one for each index of `groups`. A program takes and returns all parts, laid end to end along the dimension named above; an argument that names none is the same for every part. Nothing has to cross between parts.
All inputs are finite; a program needn't handle non-finite values.
Results may differ from a plain program's by a relative error of at most 0.0075.
Values may be sent and summed in bfloat16 or wider, within the bound.
A program may use at most 192 MiB of HBM per device.

v0:
```python
import jax
import jax.numpy as jnp
from jax import lax
from jax.sharding import PartitionSpec as P

TAYLOR = 4


def per_device(fields, chol, orbitals, trial):
    all_fields = lax.all_gather(fields, "wide", axis=0, tiled=True)
    vectors, rows, width = chol.shape
    chol_flat = chol.reshape(vectors, rows * width)
    generator = jnp.dot(all_fields, chol_flat, preferred_element_type=jnp.float32).astype(
        jnp.bfloat16
    )
    generator = generator.reshape(all_fields.shape[0], rows, width)
    owned = lax.all_to_all(generator, "wide", split_axis=0, concat_axis=1, tiled=True)
    nocc = orbitals.shape[2] // 2
    walk_local = orbitals.shape[0]
    gen_walker = owned[0]
    total = orbitals[0].astype(jnp.float32)
    operand = orbitals[0]
    for order in range(1, TAYLOR + 1):
        product = jnp.dot(gen_walker, operand, preferred_element_type=jnp.float32)
        term = jnp.concatenate([-product[:, nocc:], product[:, :nocc]], axis=1) / order
        total = total + term
        if order < TAYLOR:
            operand = term.astype(jnp.bfloat16)
    fresh_list = [total.astype(jnp.bfloat16)]
    new_orbitals = jnp.stack(fresh_list, axis=0)
    trial_real = trial[:, :nocc].T
    trial_imag = trial[:, nocc:].T
    mixer = jnp.concatenate(
        [
            jnp.concatenate([trial_real, -trial_imag], axis=1),
            jnp.concatenate([trial_imag, trial_real], axis=1),
        ],
        axis=0,
    )
    orbital_rows = lax.all_to_all(new_orbitals, "wide", split_axis=1, concat_axis=0, tiled=True)
    count = orbital_rows.shape[0]
    flat_rows = orbital_rows.reshape(count * rows, 2 * nocc)
    tile_green = jnp.dot(flat_rows, mixer, preferred_element_type=jnp.float32).astype(jnp.bfloat16)
    tile_green = tile_green.reshape(count, rows, 2 * width)
    all_walk = tile_green.shape[0]
    tile_green = (
        tile_green.reshape(all_walk, rows, 2, width)
        .transpose(0, 2, 1, 3)
        .reshape(all_walk * 2, rows * width)
    )
    partial_value = jnp.dot(tile_green, chol_flat.T, preferred_element_type=jnp.float32).reshape(
        all_walk, 2, vectors
    )
    summed = lax.psum(partial_value, "wide")
    force_bias = lax.dynamic_slice_in_dim(
        summed, lax.axis_index("wide") * walk_local, walk_local, 0
    )
    return (new_orbitals, force_bias)


def solution(mesh):
    in_specs = (
        P(("groups", "wide"), None),
        P(None, "wide", None),
        P(("groups", "wide"), None, None),
        P(),
    )
    out_specs = (P(("groups", "wide"), None, None), P(("groups", "wide"), None, None))
    return jax.shard_map(
        per_device, mesh=mesh, in_specs=in_specs, out_specs=out_specs, check_vma=False
    )
```

profile of v0, /device:TPU:0, one launch (start us, length us, event | category | flops | bytes accessed | tf_op | source)
XLA Modules:
  0.0 378.8 jit_solution(17390543338026890626)
XLA Ops:
  7.2 0.0 copy-start.2
  7.2 58.5 %copy.31 = bf16[64,8,64,1024]{3,1,2,0:T(8,128)(2,1)} copy(bf16[64,8,64,1024]{3,2,1,0:T(8,128)(2,1)} %bitcast.19) | data formatting | bytes 134217728
  65.7 0.0 copy-done.2
  65.7 23.1 %all-gather = bf16[16,1,512]{2,1,0:T(2,128)(2,1)S(1)} all-gather(bf16[1,1,512]{2,1,0:T(2,128)(2,1)S(1)} %bitcast.65), channel_id=1, replica_groups=mesh['groups'=2,'wide'=16] {'wide'}, dimensions={0}, use_global_device_ids=true | all-gather | bytes 17408 | tf_op jit(solution)/shard_map/all_gather | solution.py:10
  88.9 22.8 %convolution_convert_fusion = bf16[16,65536]{1,0:T(8,128)(2,1)S(1)} fusion(bf16[512,65536]{1,0:T(8,128)(2,1)} %bitcast.20, bf16[16,1,512]{2,1,0:T(2,128)(2,1)S(1)} %all-gather), kind=kOutput, calls=%fused_computation | convolution fusion | flops 1074790400 | bytes 69222400 | tf_op jit(solution)/shard_map/dot_general | solution.py:13
  111.6 2.5 copy.32
  114.1 0.0 copy-start
  114.1 4.0 %all-to-all-start = ((bf16[16,64,1024]{2,1,0:T(8,128)(2,1)}), bf16[16,64,1024]{2,1,0:T(8,128)(2,1)S(1)}, u32[]{:S(2)}, u32[]{:S(2)}) async-start(bf16[16,64,1024]{2,1,0:T(8,128)(2,1)} %bitcast.62), calls=%async_computation | async-start | bytes 4194304 | tf_op jit(solution)/shard_map/all_to_all | solution.py:17
  118.2 0.0 copy-done
  118.2 0.2 copy.22
  118.4 40.6 %all-to-all-done = bf16[16,64,1024]{2,1,0:T(8,128)(2,1)S(1)} async-done(((bf16[16,64,1024]{2,1,0:T(8,128)(2,1)}), bf16[16,64,1024]{2,1,0:T(8,128)(2,1)S(1)}, u32[]{:S(2)}, u32[]{:S(2)}) %all-to-all-start) | async-done | bytes 2097184 | tf_op jit(solution)/shard_map/all_to_all | solution.py:17
  159.0 0.8 fusion.34
  159.8 0.1 fusion.38
  159.9 0.7 fusion.28
  160.7 0.1 slice_negate_fusion.2
  160.8 0.8 fusion.25
  161.6 0.1 slice_negate_fusion.1
  161.8 0.7 fusion.23
  162.5 0.1 fusion.27
  162.6 0.6 fusion.13
  163.2 0.9 copy.23
  164.0 0.0 copy-start.1
  164.0 0.5 broadcast.24
  164.5 3.8 %reduce = bf16[1024,256]{1,0:T(8,128)(2,1)S(1)} reduce(bf16[1024,1,256]{2,1,0:T(2,128)(2,1)S(1)} %bitcast.63, bf16[]{:T(256)} %broadcast.24), dimensions={1}, to_apply=%bitcast.50.reduce_sub_computation | reduce | bytes 1048578
  168.4 0.9 reshape.121
  169.3 11.2 %all-to-all-start.1 = ((bf16[16,2,8192]{2,1,0:T(2,128)(2,1)}), bf16[16,2,8192]{2,1,0:T(2,128)(2,1)S(1)}, u32[]{:S(2)}, u32[]{:S(2)}) async-start(bf16[16,2,8192]{2,1,0:T(2,128)(2,1)} %reshape.121), calls=%async_computation.1 | async-start | bytes 1048576 | tf_op jit(solution)/shard_map/all_to_all | solution.py:40
  180.5 0.0 all-reduce.2.cloned.1.call-start
  180.5 0.0 copy-done.1
  180.6 14.3 %all-to-all-done.1 = bf16[16,2,8192]{2,1,0:T(2,128)(2,1)S(1)} async-done(((bf16[16,2,8192]{2,1,0:T(2,128)(2,1)}), bf16[16,2,8192]{2,1,0:T(2,128)(2,1)S(1)}, u32[]{:S(2)}, u32[]{:S(2)}) %all-to-all-start.1) | async-done | bytes 524320 | tf_op jit(solution)/shard_map/all_to_all | solution.py:40
  194.9 0.5 reshape.122
  195.5 3.3 convolution_convert_fusion.1
  198.7 7.8 %reshape_reshape.3 = bf16[16,64,2,1024]{3,2,1,0:T(2,128)(2,1)} reshape(bf16[1024,2048]{1,0:T(8,128)(2,1)} %convolution_convert_fusion.1) | data formatting | bytes 8388608 | tf_op jit(solution)/shard_map/reshape;reshape | solution.py:47
  206.5 80.0 %fusion.5 = f32[16,2,512]{2,0,1:T(8,128)} fusion(bf16[512,64,1024]{2,1,0:T(8,128)(2,1)} %param.5, bf16[16,64,2,1024]{3,2,1,0:T(2,128)(2,1)} %reshape_reshape.3), kind=kOutput, calls=%fused_computation.7 | convolution fusion | flops 2147483648 | bytes 71368704 | tf_op jit(solution)/shard_map/dot_general | solution.py:51
  286.5 0.0 all-reduce.2.cloned.1.call-update
  286.5 1.0 copy.26
  287.5 83.0 %all-reduce.2.cloned.1.call-done = f32[16,2,512]{2,0,1:T(8,128)} async-done(((f32[16,2,512]{2,0,1:T(8,128)}), f32[16,2,512]{2,0,1:T(8,128)}) %all-reduce.2.cloned.1.call-update) | async-done | bytes 65552 | tf_op jit(solution)/shard_map/psum | solution.py:54
  370.6 0.8 constant_dynamic-slice_fusion
  371.3 0.6 copy.27
  (3 shorter events, 0.1 us)
Async XLA Ops:
  7.2 58.6 %copy-start.2 = (bf16[1,512]{1,0:T(2,128)(2,1)S(1)}, bf16[1,512]{1,0:T(2,128)(2,1)}, u32[]{:S(2)}) copy-start(bf16[1,512]{1,0:T(2,128)(2,1)} %param.4) | copy-start | bytes 3076
  114.1 4.0 %copy-start = (bf16[1,1024,256]{2,1,0:T(8,128)(2,1)S(1)}, bf16[1,1024,256]{2,1,0:T(8,128)(2,1)}, u32[]{:S(2)}) copy-start(bf16[1,1024,256]{2,1,0:T(8,128)(2,1)} %param.6) | copy-start | bytes 1572868
  114.1 44.9 %all-to-all-start = ((bf16[16,64,1024]{2,1,0:T(8,128)(2,1)}), bf16[16,64,1024]{2,1,0:T(8,128)(2,1)S(1)}, u32[]{:S(2)}, u32[]{:S(2)}) async-start(bf16[16,64,1024]{2,1,0:T(8,128)(2,1)} %bitcast.62), calls=%async_computation | async-start | bytes 4194304 | tf_op jit(solution)/shard_map/all_to_all | solution.py:17
  164.0 16.5 %copy-start.1 = (bf16[1024,256]{1,0:T(8,128)(2,1)S(1)}, bf16[1024,256]{1,0:T(8,128)(2,1)}, u32[]{:S(2)}) copy-start(bf16[1024,256]{1,0:T(8,128)(2,1)} %param.7) | copy-start | bytes 1572868
  169.3 25.6 %all-to-all-start.1 = ((bf16[16,2,8192]{2,1,0:T(2,128)(2,1)}), bf16[16,2,8192]{2,1,0:T(2,128)(2,1)S(1)}, u32[]{:S(2)}, u32[]{:S(2)}) async-start(bf16[16,2,8192]{2,1,0:T(2,128)(2,1)} %reshape.121), calls=%async_computation.1 | async-start | bytes 1048576 | tf_op jit(solution)/shard_map/all_to_all | solution.py:40
  180.5 190.1 %all-reduce.2.cloned.1.call-start = ((), (), s32[]{:S(2)}) async-start(), calls=%async_computation.2 | async-start | bytes 131072 | tf_op jit(solution)/shard_map/psum | solution.py:54
Sparse Core Ops, SparseCore 0:
  286.6 83.8 all-reduce.1
where the time goes:
time: 380 us; the launch traced here: 379 us
  waiting for transfers between devices  138 us (36%)
  matrix products  109 us (29%)
  local copies, waits for them, and re-layouts  74.3 us (20%)
  blocking collectives  23.1 us (6%)
  starting transfers between devices  15.2 us (4%)
  between operations  14.2 us (4%)
  other arithmetic  4.9 us (1%)
    psum x1, waiting for transfers between devices, per_device(): summed = lax.psum(partial_value, 'wide')  83 us
    dot_general x1, matrix products, per_device(): jnp.dot(tile_green, chol_flat.T, preferred_element_type=jnp.float32)  80 us
    unnamed x14, local copies, waits for them, and re-layouts  64.8 us
    all_to_all x1, waiting for transfers between devices, per_device(): lax.all_to_all(generator, 'wide', split_axis=0, concat_axis=1, tiled=True)  40.6 us
    all_gather x1, blocking collectives, per_device(): all_fields = lax.all_gather(fields, 'wide', axis=0, tiled=True)  23.1 us
    dot_general x1, matrix products, per_device(): jnp.dot(all_fields, chol_flat, preferred_element_type=jnp.float32)  22.8 us
    all_to_all x1, waiting for transfers between devices, per_device(): lax.all_to_all(new_orbitals, 'wide', split_axis=1, concat_axis=0, tiled=T...  14.3 us
    all_to_all x1, starting transfers between devices, per_device(): lax.all_to_all(new_orbitals, 'wide', split_axis=1, concat_axis=0, tiled=T...  11.2 us
  transfers between devices with their start and end apart: 3, of which 3 were waited for; matrix products, arithmetic and copies ran while one was open for 0% of the time, Pallas kernels for 0%

commit v1 on v0

v1 whole, which is shorter than its diff:
```python
import functools

import jax
import jax.numpy as jnp
from jax import lax
from jax.experimental import pallas as pl
from jax.experimental.pallas import tpu as pltpu
from jax.sharding import PartitionSpec as P

TAYLOR = 4
SUB = 8
LANES = 128
MESH = pl.DeviceIdType.MESH
NT = (((1,), (1,)), ((), ()))


def kernel(
    n, halves, slots, row_block,
    fld, chol, orb, trial, out, bias,
    fall, kron, held, accum, gen_local, gen_all, total, operand, orb_rows, orb_wide,
    green, scores, fb, fb_all, load_sem, send_sem, recv_sem,
):
    me = lax.axis_index("wide")
    vectors, rows, width = chol.shape
    half_vectors = vectors // halves
    units = (rows // row_block) * halves
    subs = row_block // SUB
    walkers = n
    depth = half_vectors * SUB
    cols = 256
    groups_q = vectors // LANES

    def load(unit):
        b, gh = unit // halves, lax.rem(unit, halves)
        return pltpu.make_async_copy(
            chol.at[pl.ds(gh * half_vectors, half_vectors), pl.ds(b * row_block, row_block), :],
            held.at[lax.rem(unit, slots)],
            load_sem.at[lax.rem(unit, slots)],
        )

    def start_load(unit, _=None):
        load(unit).start()

    def peers(body):
        lax.fori_loop(1, n, lambda k, c: (body(lax.rem(me + k, n)), c)[1], 0)

    def send(src, dst, which, peer):
        pltpu.make_async_remote_copy(
            src_ref=src, dst_ref=dst, send_sem=send_sem.at[which], recv_sem=recv_sem.at[which],
            device_id={"wide": peer}, device_id_type=MESH,
        ).start()

    def wait_all(ref, sem):
        part = ref.at[pl.ds(0, n - 1)]
        pltpu.make_async_copy(part, part, sem).wait()

    lax.fori_loop(0, slots, lambda u, c: (start_load(u), c)[1], 0)

    barrier = pltpu.get_barrier_semaphore()
    peers(lambda p: pl.semaphore_signal(barrier, inc=1, device_id={"wide": p}, device_id_type=MESH))
    pl.semaphore_wait(barrier, n - 1)

    peers(lambda p: send(fld, fall.at[me], 0, p))
    fall[me] = fld[...]
    wait_all(fall, recv_sem.at[0])

    span = LANES * SUB
    spread = (
        lax.broadcasted_iota(jnp.int32, (LANES, span), 1) >> 3
        == lax.broadcasted_iota(jnp.int32, (LANES, span), 0)
    ).astype(jnp.bfloat16)
    diagonal = (lax.broadcasted_iota(jnp.int32, (walkers * SUB, span), 1) & (SUB - 1)) == (
        lax.broadcasted_iota(jnp.int32, (walkers * SUB, span), 0) & (SUB - 1)
    )
    for q in range(groups_q):
        line = jnp.broadcast_to(fall[:, q : q + 1, :], (walkers, SUB, LANES))
        line = line.reshape(walkers * SUB, LANES).astype(jnp.bfloat16)
        wide = jnp.dot(line, spread, preferred_element_type=jnp.float32)
        kron[:, q * span : (q + 1) * span] = jnp.where(diagonal, wide, 0.0).astype(jnp.bfloat16)

    def generate(unit, carry):
        b, gh = unit // halves, lax.rem(unit, halves)
        slot = lax.rem(unit, slots)
        load(unit).wait()

        @pl.when(gh == 0)
        def _():
            accum[...] = jnp.zeros_like(accum)

        for h in range(subs):

            def column(jc, c):
                at = pl.ds(pl.multiple_of(jc * cols, cols), cols)
                right = held[slot, :, h * SUB : (h + 1) * SUB, at].reshape(depth, cols)
                left = kron[:, pl.ds(pl.multiple_of(gh * depth, depth), depth)]
                got = jnp.dot(left, right, preferred_element_type=jnp.float32)
                accum[:, h * SUB : (h + 1) * SUB, at] += got.reshape(walkers, SUB, cols)
                return c

            lax.fori_loop(0, width // cols, column, 0)

        @pl.when(unit + slots < units)
        def _():
            start_load(unit + slots)

        @pl.when(gh == halves - 1)
        def _():
            at = pl.ds(pl.multiple_of(b * row_block, row_block), row_block)
            gen_local[:, at, :] = accum[...].astype(jnp.bfloat16)
            peers(lambda p: send(gen_local.at[p, at], gen_all.at[me, at], 1, p))
            gen_all[me, at, :] = gen_local[me, at, :]

        return carry

    lax.fori_loop(0, units, generate, 0)

    scores[...] = jnp.zeros_like(scores)
    fb[...] = jnp.zeros_like(fb)
    wait_all(gen_all, recv_sem.at[1])

    size = orb.shape[0]
    nocc = orb.shape[1] // 2
    tile = 256
    per_tile = tile // rows
    for order in range(1, TAYLOR + 1):

        def advance(i, c, order=order):
            at = pl.ds(pl.multiple_of(i * tile, tile), tile)
            gen = gen_all[pl.ds(i * per_tile, per_tile), :, :].reshape(tile, size)
            before = orb[...] if order == 1 else operand[order % 2]
            product = jnp.dot(gen, before, preferred_element_type=jnp.float32)
            term = jnp.concatenate([-product[:, nocc:], product[:, :nocc]], axis=1) / order
            if order == 1:
                now = orb[at, :].astype(jnp.float32) + term
            else:
                now = total[at, :] + term
            if order < TAYLOR:
                total[at, :] = now
                operand[(order + 1) % 2, at, :] = term.astype(jnp.bfloat16)
            else:
                out[pl.ds(i * per_tile, per_tile), :, :] = now.reshape(
                    per_tile, rows, 2 * nocc
                ).astype(jnp.bfloat16)
            return c

        lax.fori_loop(0, size // tile, advance, 0)

    peers(lambda p: send(out.at[p], orb_rows.at[me], 2, p))
    orb_rows[me] = out[me]
    wait_all(orb_rows, recv_sem.at[2])

    orb_wide[...] = orb_rows[...].astype(jnp.float32)

    def make_green(r, c):
        at = pl.ds(pl.multiple_of(r * SUB, SUB), SUB)
        block = orb_wide[:, at, :].reshape(walkers * SUB, 2 * nocc)
        turned = jnp.concatenate([block[:, nocc:], -block[:, :nocc]], axis=1)
        both = jnp.concatenate([block, turned], axis=0).astype(jnp.bfloat16)
        green[r] = lax.dot_general(
            trial[...], both, NT, preferred_element_type=jnp.float32
        ).astype(jnp.bfloat16)
        return c

    lax.fori_loop(0, rows // SUB, make_green, 0)

    chunk = 64
    many = 2 * walkers * SUB
    take = min(many, 256)
    for nc in range(many // take):
        if nc:
            scores[...] = jnp.zeros_like(scores)

        def contract(step, carry, nc=nc):
            unit = lax.rem(units - slots + step, units)
            b, gh = unit // halves, lax.rem(unit, halves)
            slot = lax.rem(unit, slots)

            if slots < units:

                @pl.when(step >= slots)
                def _():
                    load(unit).wait()

            def piece(i, c):
                got = None
                for h in range(subs):
                    left = held[slot, pl.ds(i * chunk, chunk), h * SUB : (h + 1) * SUB, :]
                    add = jnp.dot(
                        left.reshape(chunk * SUB, width),
                        green[b * subs + h, :, nc * take : (nc + 1) * take],
                        preferred_element_type=jnp.float32,
                    )
                    got = add if got is None else got + add
                at = pl.ds(pl.multiple_of(gh * depth + i * chunk * SUB, SUB), chunk * SUB)
                scores[at, :] += got
                return c

            lax.fori_loop(0, half_vectors // chunk, piece, 0)

            if slots < units:

                @pl.when(step + slots < units)
                def _():
                    start_load(step)

            return carry

        lax.fori_loop(0, units, contract, 0)

        own = (lax.broadcasted_iota(jnp.int32, (SUB, take), 1) & (SUB - 1)) == (
            lax.broadcasted_iota(jnp.int32, (SUB, take), 0)
        )
        lines = fb.shape[1]
        walker = lax.broadcasted_iota(jnp.int32, (walkers, lines, take), 0)
        line = lax.broadcasted_iota(jnp.int32, (walkers, lines, take), 1)
        source = (lax.broadcasted_iota(jnp.int32, (walkers, lines, take), 2) + nc * take) >> 3
        for q in range(groups_q):
            part = scores[q * span : (q + 1) * span, :].reshape(LANES, SUB, take)
            part = jnp.sum(jnp.where(own[None], part, 0.0), axis=1)
            pick = ((line == q) & (source == walker)) | (
                (line == groups_q + q) & (source == walkers + walker)
            )
            pick = pick.astype(jnp.float32).reshape(walkers * lines, take)
            fb[...] += lax.dot_general(
                pick, part, NT, preferred_element_type=jnp.float32, precision=lax.Precision.HIGHEST
            ).reshape(walkers, lines, LANES)

    peers(lambda p: send(fb.at[p], fb_all.at[me], 3, p))
    fb_all[me] = fb[me]
    wait_all(fb_all, recv_sem.at[3])
    bias[...] = jnp.sum(fb_all[...], axis=0)

    wait_all(fall, send_sem.at[0])
    wait_all(gen_local, send_sem.at[1])
    wait_all(orb_rows, send_sem.at[2])
    wait_all(fb, send_sem.at[3])


def per_device(n, fields, chol, orbitals, trial):
    vectors, rows, width = chol.shape
    size, both = orbitals.shape[1:]
    row_block = min(16, rows)
    halves = 2
    units = (rows // row_block) * halves
    slots = min(4, units)
    q = vectors // LANES
    lines = -(-q // 8) * 8
    fb_lines = -(-2 * q // 8) * 8
    fld = jnp.pad(fields.astype(jnp.float32).reshape(q, LANES), ((0, lines - q), (0, 0)))
    vmem = pl.BlockSpec(memory_space=pltpu.VMEM)
    bf16, f32 = jnp.bfloat16, jnp.float32
    out, bias = pl.pallas_call(
        functools.partial(kernel, n, halves, slots, row_block),
        out_shape=(
            jax.ShapeDtypeStruct((n, rows, both), bf16),
            jax.ShapeDtypeStruct((fb_lines, LANES), f32),
        ),
        in_specs=[vmem, pl.BlockSpec(memory_space=pl.ANY), vmem, vmem],
        out_specs=(vmem, vmem),
        scratch_shapes=[
            pltpu.VMEM((n, lines, LANES), f32),
            pltpu.VMEM((n * SUB, vectors * SUB), bf16),
            pltpu.VMEM((slots, vectors // halves, row_block, width), bf16),
            pltpu.VMEM((n, row_block, width), f32),
            pltpu.VMEM((n, rows, width), bf16),
            pltpu.VMEM((n, rows, width), bf16),
            pltpu.VMEM((size, both), f32),
            pltpu.VMEM((2, size, both), bf16),
            pltpu.VMEM((n, rows, both), bf16),
            pltpu.VMEM((n, rows, both), f32),
            pltpu.VMEM((rows // SUB, width, 2 * n * SUB), bf16),
            pltpu.VMEM((vectors * SUB, min(2 * n * SUB, 256)), f32),
            pltpu.VMEM((n, fb_lines, LANES), f32),
            pltpu.VMEM((n, fb_lines, LANES), f32),
            pltpu.SemaphoreType.DMA((slots,)),
            pltpu.SemaphoreType.DMA((4,)),
            pltpu.SemaphoreType.DMA((4,)),
        ],
        compiler_params=pltpu.CompilerParams(
            collective_id=0, has_side_effects=True, vmem_limit_bytes=60 * 1024 * 1024
        ),
    )(fld, chol, orbitals[0], trial)
    return (
        out.reshape(1, size, both),
        bias[: 2 * q].reshape(1, 2, vectors),
    )


def solution(mesh):
    in_specs = (
        P(("groups", "wide"), None),
        P(None, "wide", None),
        P(("groups", "wide"), None, None),
        P(),
    )
    out_specs = (P(("groups", "wide"), None, None), P(("groups", "wide"), None, None))
    return jax.shard_map(
        functools.partial(per_device, mesh.shape["wide"]),
        mesh=mesh, in_specs=in_specs, out_specs=out_specs, check_vma=False,
    )
```

time: 380 us -> 120 us (0.32)
  waiting for transfers between devices: 138 us -> 0 us
  Pallas kernels: 0 us -> 114 us
  matrix products: 109 us -> 0 us
  local copies, waits for them, and re-layouts: 74.3 us -> 3.15 us
  blocking collectives: 23.1 us -> 0 us
  starting transfers between devices: 15.2 us -> 0 us
  between operations: 14.2 us -> 0.64 us
    pallas_call x0 -> x1, Pallas kernels: none -> 114 us  [per_device(): pl.pallas_call(functools.partial(kernel, n, halves, slots, row_block), ou...]
    dot_general x7 -> x0, matrix products: 109 us -> none  [the longest x1 80 us: per_device(): jnp.dot(tile_green, chol_flat.T, preferred_element_type=jnp.float32)]
    psum x1 -> x0, waiting for transfers between devices: 83 us -> none  [per_device(): summed = lax.psum(partial_value, 'wide')]
    unnamed x14 -> x1, local copies, waits for them, and re-layouts: 64.8 us -> 1.87 us
    all_to_all x2 -> x0, waiting for transfers between devices: 54.9 us -> none  [the longest x1 40.6 us: per_device(): lax.all_to_all(generator, 'wide', split_axis=0, concat_axis=1, tiled=True)]
    all_gather x1 -> x0, blocking collectives: 23.1 us -> none  [per_device(): all_fields = lax.all_gather(fields, 'wide', axis=0, tiled=True)]
    all_to_all x2 -> x0, starting transfers between devices: 15.2 us -> none  [the longest x1 11.2 us: per_device(): lax.all_to_all(new_orbitals, 'wide', split_axis=1, concat_axis=0, tiled=T...]
    another operation x1 -> x0, local copies, waits for them, and re-layouts: 7.78 us -> none  [per_device(): tile_green.reshape(all_walk, rows, 2, width).transpose(0, 2, 1, 3)]
  transfers between devices with their start and end apart: 3 -> 0, of which waited for: 3 -> 0; matrix products, arithmetic and copies ran while one was open for 0% -> 0% of each run, Pallas kernels for 0% -> 0%
where the time goes in v1:
time: 120 us; the launch traced here: 119 us
  Pallas kernels  114 us (95%)
  local copies, waits for them, and re-layouts  3.15 us (3%)
  other arithmetic  1.3 us (1%)
    pallas_call x1, Pallas kernels, per_device(): pl.pallas_call(functools.partial(kernel, n, halves, slots, row_block), ou...  114 us

profile of v1, /device:TPU:0, one launch (start us, length us, event | category | flops | bytes accessed | tf_op | source)
XLA Modules:
  0.0 119.3 jit_solution(15207327528811374948)
XLA Ops:
  0.6 0.7 reduce
  1.3 0.6 pad_convert_fusion.fld
  1.9 114.2 %shard_map.59 = (bf16[16,64,256]{2,1,0:T(8,128)(2,1)}, f32[8,128]{1,0:T(8,128)}) custom-call(f32[8,128]{1,0:T(8,128)} %pad_convert_fusion.fld, bf16[512,64,1024]{2,1,0:T(8,128)(2,1)} %chol.1, bf16[1024,256]{1,0:T(8,128)(2,1)} %bitcast.3, bf16[1024,256]{1,0:T(8,128)(2,1)} %trial.1), custom_call_target="tpu_custom_call" | custom-call | tf_op jit(solution)/shard_map/pallas_call | solution.py:252
  116.2 1.3 %reshape.16 = f32[1,2,512]{2,1,0:T(2,128)} reshape(f32[8,128]{1,0:T(8,128)} %get-tuple-element.5) | data formatting | bytes 8192 | tf_op jit(solution)/shard_map/reshape | solution.py:285
  117.4 1.9 %copy.7 = bf16[1,1024,256]{2,1,0:T(8,128)(2,1)} copy(bf16[1,1024,256]{2,1,0:T(8,128)(2,1)} %bitcast.4) | data formatting | bytes 1048576

commit v2 on v1

--- a/solution.py
+++ b/solution.py
@@ -16,9 +16,9 @@
 
 def kernel(
     n, halves, slots, row_block,
-    fld, chol, orb, trial, out, bias,
-    fall, kron, held, accum, gen_local, gen_all, total, operand, orb_rows, orb_wide,
-    green, scores, fb, fb_all, load_sem, send_sem, recv_sem,
+    fields, chol, orb, trial, out, bias,
+    fld, fall, kron, held, accum, gen_local, gen_all, total, operand, orb_rows, orb_wide,
+    green, scores, fb, fb_all, load_sem, send_sem, recv_sem, orb_sem,
 ):
     me = lax.axis_index("wide")
     vectors, rows, width = chol.shape
@@ -44,9 +44,17 @@
     def peers(body):
         lax.fori_loop(1, n, lambda k, c: (body(lax.rem(me + k, n)), c)[1], 0)
 
-    def send(src, dst, which, peer):
+    def far_first(body):
+        half = n // 2
+        side = me // half
+        across, here = (1 - side) * half, side * half
+        lax.fori_loop(0, half, lambda k, c: (body(across + lax.rem(me + k, half)), c)[1], 0)
+        lax.fori_loop(1, half, lambda k, c: (body(here + lax.rem(me + k, half)), c)[1], 0)
+
+    def send(src, dst, which, peer, arrived=None):
         pltpu.make_async_remote_copy(
-            src_ref=src, dst_ref=dst, send_sem=send_sem.at[which], recv_sem=recv_sem.at[which],
+            src_ref=src, dst_ref=dst, send_sem=send_sem.at[which],
+            recv_sem=recv_sem.at[which] if arrived is None else arrived,
             device_id={"wide": peer}, device_id_type=MESH,
         ).start()
 
@@ -60,6 +68,9 @@
     peers(lambda p: pl.semaphore_signal(barrier, inc=1, device_id={"wide": p}, device_id_type=MESH))
     pl.semaphore_wait(barrier, n - 1)
 
+    fld[...] = jnp.zeros_like(fld)
+    for q in range(groups_q):
+        fld[q : q + 1, :] = fields[:, q * LANES : (q + 1) * LANES].astype(jnp.float32)
     peers(lambda p: send(fld, fall.at[me], 0, p))
     fall[me] = fld[...]
     wait_all(fall, recv_sem.at[0])
@@ -107,7 +118,7 @@
         def _():
             at = pl.ds(pl.multiple_of(b * row_block, row_block), row_block)
             gen_local[:, at, :] = accum[...].astype(jnp.bfloat16)
-            peers(lambda p: send(gen_local.at[p, at], gen_all.at[me, at], 1, p))
+            far_first(lambda p: send(gen_local.at[p, at], gen_all.at[me, at], 1, p))
             gen_all[me, at, :] = gen_local[me, at, :]
 
         return carry
@@ -145,23 +156,26 @@
 
         lax.fori_loop(0, size // tile, advance, 0)
 
-    peers(lambda p: send(out.at[p], orb_rows.at[me], 2, p))
+    blocks = rows // row_block
+    first = (units - slots) // halves
+    for step in range(blocks):
+        b = (first + step) % blocks
+        at = pl.ds(b * row_block, row_block)
+        far_first(lambda p, at=at, b=b: send(out.at[p, at], orb_rows.at[me, at], 2, p, orb_sem.at[b]))
     orb_rows[me] = out[me]
-    wait_all(orb_rows, recv_sem.at[2])
-
-    orb_wide[...] = orb_rows[...].astype(jnp.float32)
-
-    def make_green(r, c):
-        at = pl.ds(pl.multiple_of(r * SUB, SUB), SUB)
-        block = orb_wide[:, at, :].reshape(walkers * SUB, 2 * nocc)
-        turned = jnp.concatenate([block[:, nocc:], -block[:, :nocc]], axis=1)
-        both = jnp.concatenate([block, turned], axis=0).astype(jnp.bfloat16)
-        green[r] = lax.dot_general(
-            trial[...], both, NT, preferred_element_type=jnp.float32
-        ).astype(jnp.bfloat16)
-        return c
-
-    lax.fori_loop(0, rows // SUB, make_green, 0)
+
+    def make_green(b):
+        at = pl.ds(pl.multiple_of(b * row_block, row_block), row_block)
+        part = orb_rows.at[pl.ds(0, n - 1), at]
+        pltpu.make_async_copy(part, part, orb_sem.at[b]).wait()
+        orb_wide[...] = orb_rows[:, at, :].astype(jnp.float32)
+        for h in range(subs):
+            block = orb_wide[:, h * SUB : (h + 1) * SUB, :].reshape(walkers * SUB, 2 * nocc)
+            turned = jnp.concatenate([block[:, nocc:], -block[:, :nocc]], axis=1)
+            both = jnp.concatenate([block, turned], axis=0).astype(jnp.bfloat16)
+            green[b * subs + h] = lax.dot_general(
+                trial[...], both, NT, preferred_element_type=jnp.float32
+            ).astype(jnp.bfloat16)
 
     chunk = 64
     many = 2 * walkers * SUB
@@ -174,6 +188,12 @@
             unit = lax.rem(units - slots + step, units)
             b, gh = unit // halves, lax.rem(unit, halves)
             slot = lax.rem(unit, slots)
+
+            if nc == 0:
+
+                @pl.when(gh == 0)
+                def _():
+                    make_green(b)
 
             if slots < units:
 
@@ -228,7 +248,12 @@
     peers(lambda p: send(fb.at[p], fb_all.at[me], 3, p))
     fb_all[me] = fb[me]
     wait_all(fb_all, recv_sem.at[3])
-    bias[...] = jnp.sum(fb_all[...], axis=0)
+    summed = jnp.sum(fb_all[...], axis=0)
+    for q in range(groups_q):
+        for c in range(2):
+            bias[c : c + 1, q * LANES : (q + 1) * LANES] = summed[
+                c * groups_q + q : c * groups_q + q + 1
+            ]
 
     wait_all(fall, send_sem.at[0])
     wait_all(gen_local, send_sem.at[1])
@@ -246,18 +271,18 @@
     q = vectors // LANES
     lines = -(-q // 8) * 8
     fb_lines = -(-2 * q // 8) * 8
-    fld = jnp.pad(fields.astype(jnp.float32).reshape(q, LANES), ((0, lines - q), (0, 0)))
     vmem = pl.BlockSpec(memory_space=pltpu.VMEM)
     bf16, f32 = jnp.bfloat16, jnp.float32
     out, bias = pl.pallas_call(
         functools.partial(kernel, n, halves, slots, row_block),
         out_shape=(
             jax.ShapeDtypeStruct((n, rows, both), bf16),
-            jax.ShapeDtypeStruct((fb_lines, LANES), f32),
+            jax.ShapeDtypeStruct((2, vectors), f32),
         ),
         in_specs=[vmem, pl.BlockSpec(memory_space=pl.ANY), vmem, vmem],
         out_specs=(vmem, vmem),
         scratch_shapes=[
+            pltpu.VMEM((lines, LANES), f32),
             pltpu.VMEM((n, lines, LANES), f32),
             pltpu.VMEM((n * SUB, vectors * SUB), bf16),
             pltpu.VMEM((slots, vectors // halves, row_block, width), bf16),
@@ -267,7 +292,7 @@
             pltpu.VMEM((size, both), f32),
             pltpu.VMEM((2, size, both), bf16),
             pltpu.VMEM((n, rows, both), bf16),
-            pltpu.VMEM((n, rows, both), f32),
+            pltpu.VMEM((n, row_block, both), f32),
             pltpu.VMEM((rows // SUB, width, 2 * n * SUB), bf16),
             pltpu.VMEM((vectors * SUB, min(2 * n * SUB, 256)), f32),
             pltpu.VMEM((n, fb_lines, LANES), f32),
@@ -275,14 +300,15 @@
             pltpu.SemaphoreType.DMA((slots,)),
             pltpu.SemaphoreType.DMA((4,)),
             pltpu.SemaphoreType.DMA((4,)),
+            pltpu.SemaphoreType.DMA((rows // row_block,)),
         ],
         compiler_params=pltpu.CompilerParams(
             collective_id=0, has_side_effects=True, vmem_limit_bytes=60 * 1024 * 1024
         ),
-    )(fld, chol, orbitals[0], trial)
+    )(fields, chol, orbitals[0], trial)
     return (
         out.reshape(1, size, both),
-        bias[: 2 * q].reshape(1, 2, vectors),
+        bias.reshape(1, 2, vectors),
     )
 
 

time: 120 us -> 111 us (0.925)
  Pallas kernels: 114 us -> 107 us
  other arithmetic: 1.3 us -> 0 us
    pallas_call x1, Pallas kernels: 114 us -> 107 us  [per_device(): pl.pallas_call(functools.partial(kernel, n, halves, slots, row_block), ou...]
    reshape x1 -> x0, local copies, waits for them, and re-layouts: 1.28 us -> none  [per_device(): return (out.reshape(1, size, both), bias[:2 * q].reshape(1, 2, vectors))]
    unnamed x1 -> x2, local copies, waits for them, and re-layouts: 1.87 us -> 3.13 us
where the time goes in v2:
time: 111 us; the launch traced here: 110 us
  Pallas kernels  107 us (96%)
  local copies, waits for them, and re-layouts  3.13 us (3%)
    pallas_call x1, Pallas kernels, per_device(): pl.pallas_call(functools.partial(kernel, n, halves, slots, row_block), ou...  107 us
    unnamed x2, local copies, waits for them, and re-layouts  3.13 us

profile of v2, /device:TPU:0, one launch (start us, length us, event | category | flops | bytes accessed | tf_op | source)
XLA Modules:
  0.0 110.4 jit_solution(11304605602298142962)
XLA Ops:
  0.6 106.7 %shard_map.59 = (bf16[16,64,256]{2,1,0:T(8,128)(2,1)}, f32[2,512]{1,0:T(2,128)}) custom-call(bf16[1,512]{1,0:T(2,128)(2,1)} %fields.1, bf16[512,64,1024]{2,1,0:T(8,128)(2,1)} %chol.1, bf16[1024,256]{1,0:T(8,128)(2,1)} %bitcast.3, bf16[1024,256]{1,0:T(8,128)(2,1)} %trial.1), custom_call_target="tpu_custom_call" | custom-call | tf_op jit(solution)/shard_map/pallas_call | solution.py:276
  107.3 1.9 %copy.8 = bf16[1,1024,256]{2,1,0:T(8,128)(2,1)} copy(bf16[1,1024,256]{2,1,0:T(8,128)(2,1)} %bitcast.4) | data formatting | bytes 1048576
  109.2 1.3 %copy.9 = f32[1,2,512]{2,1,0:T(2,128)} copy(f32[1,2,512]{2,1,0:T(2,128)} %bitcast.5) | data formatting | bytes 8192
